TPU v7x, 32 devices: a whole 2x2x4 slice. The times are simulated.
32 devices in a mesh: rep: 4 (over y, x), shard: 8 (over z, core).
Axes of the slice: x: 2, y: 2, z: 4, core: 2. Of those that a mesh axis runs over, the one named last changes fastest.
Arguments:
- tokens: bfloat16 [32768, 768], P(('rep', 'shard')), may hold values from -6 to 6
- cotangent: bfloat16 [32768, 768], P(('rep', 'shard')), may hold values from -6 to 6
- deletion: int32 [128, 256], P(('rep', 'shard')), may hold values 0 or 1
- lengths: int32 [128], P(('rep', 'shard')), may hold values from 64 to 256, as said below
- qkv_weight: float32 [768, 2304], P('shard'), may hold values from -0.21875 to 0.21875
- out_weight: float32 [768, 768], P('shard'), may hold values from -0.875 to 0.875
- up_weight: float32 [768, 3072], P('shard'), may hold values from -0.21875 to 0.21875
- down_weight: float32 [3072, 768], P('shard'), may hold values from -0.109375 to 0.109375
- vectors: float32 [12, 768], P(None, 'shard'), may hold values from -2 to 2
- qkv_first: float32 [768, 2304], P('shard'), may hold values from -192 to 192
- out_first: float32 [768, 768], P('shard'), may hold values from -192 to 192
- up_first: float32 [768, 3072], P('shard'), may hold values from -192 to 192
- down_first: float32 [3072, 768], P('shard'), may hold values from -192 to 192
- vector_first: float32 [12, 768], P(None, 'shard'), may hold values from -192 to 192
- qkv_second: float32 [768, 2304], P('shard'), may hold values from 10 to 100000
- out_second: float32 [768, 768], P('shard'), may hold values from 10 to 100000
- up_second: float32 [768, 3072], P('shard'), may hold values from 10 to 100000
- down_second: float32 [3072, 768], P('shard'), may hold values from 10 to 100000
- vector_second: float32 [12, 768], P(None, 'shard'), may hold values from 10 to 100000
Outputs:
- output: bfloat16 [32768, 768], P(('rep', 'shard'))
- token_grad: bfloat16 [32768, 768], P(('rep', 'shard'))
- qkv_grad: float32 [768, 2304], P('shard')
- out_grad: float32 [768, 768], P('shard')
- up_grad: float32 [768, 3072], P('shard')
- down_grad: float32 [3072, 768], P('shard')
- vector_grad: float32 [12, 768], P(None, 'shard')
- qkv_step: float32 [768, 2304], P('shard')
- out_step: float32 [768, 768], P('shard')
- up_step: float32 [768, 3072], P('shard')
- down_step: float32 [3072, 768], P('shard')
- vector_step: float32 [12, 768], P(None, 'shard')
- qkv_first_new: float32 [768, 2304], P('shard')
- out_first_new: float32 [768, 768], P('shard')
- up_first_new: float32 [768, 3072], P('shard')
- down_first_new: float32 [3072, 768], P('shard')
- vector_first_new: float32 [12, 768], P(None, 'shard')
Inputs may be any that keep to these rules, and one draw needn't show every extreme that they name: `lengths`: in every draw some crop has all 256 positions in use and another only 64.
All inputs are finite; a program needn't handle non-finite values. No bound on the sum of `deletion` on one device may be relied on, other than what follows from the above.
Results may differ from a plain program's by a relative error of at most 0.015.
The roundings to bfloat16 on the way count: a program that leaves them out, or rounds other values in their place, can miss the bound.
Values may be sent and summed in bfloat16 or wider, within the bound.
A program may use at most 256 MiB of HBM per device.

v0:
```python
from functools import partial
import math
import jax
import jax.numpy as jnp
from jax import lax
from jax.sharding import PartitionSpec as P

D = 768
H = 12
FF = 3072
CROP = 256
norm_epsilon = 1e-06
decay_first = 0.9
decay_second = 0.999
correct_first = 1.0 - 2.6561398887587544e-05
correct_second = 0.0952078528862904
adam_epsilon = 1e-08


def layer_norm(hidden, gain_row, shift_row):
    average = jnp.mean(hidden, axis=-1, keepdims=True)
    centred = hidden - average
    variance = jnp.mean(centred * centred, axis=-1, keepdims=True)
    inverse_root = lax.rsqrt(variance + norm_epsilon)
    normed = centred * inverse_root
    return (normed * gain_row + shift_row, normed, inverse_root)


def norm_back(grad_output, normed, inverse_root, gain_row):
    grad_normed = grad_output * gain_row
    grad_input = inverse_root * (
        grad_normed
        - jnp.mean(grad_normed, axis=-1, keepdims=True)
        - normed * jnp.mean(grad_normed * normed, axis=-1, keepdims=True)
    )
    return (grad_input, jnp.sum(grad_output * normed, axis=0), jnp.sum(grad_output, axis=0))


def attend_block(pieces):
    packed, allowed_block = pieces
    score_scale = 1.0 / math.sqrt(packed.shape[-1])
    queries = packed[:, :, 0]
    keys_in = packed[:, :, 1]
    values = packed[:, :, 2]
    scores = (
        jnp.einsum("clhd,cmhd->chlm", queries, keys_in, preferred_element_type=jnp.float32)
        * score_scale
    )
    scores = jnp.where(allowed_block[:, None, None, :], scores, -1e30)
    row_top = jnp.max(scores, axis=-1, keepdims=True)
    log_totals = row_top + jnp.log(jnp.sum(jnp.exp(scores - row_top), axis=-1, keepdims=True))
    probs_low = jnp.exp(scores - log_totals).astype(jnp.bfloat16)
    mixed_rows = jnp.einsum(
        "chlm,cmhd->clhd", probs_low, values, preferred_element_type=jnp.float32
    )
    return (mixed_rows, log_totals[..., 0])


def attend_back(pieces):
    packed, allowed_block, log_totals, grad_mixed = pieces
    score_scale = 1.0 / math.sqrt(packed.shape[-1])
    queries = packed[:, :, 0]
    keys_in = packed[:, :, 1]
    values = packed[:, :, 2]
    scores = (
        jnp.einsum("clhd,cmhd->chlm", queries, keys_in, preferred_element_type=jnp.float32)
        * score_scale
    )
    scores = jnp.where(allowed_block[:, None, None, :], scores, -1e30)
    soft_probs = jnp.exp(scores - log_totals[..., None])
    grad_probs = jnp.einsum(
        "clhd,cmhd->chlm", grad_mixed, values, preferred_element_type=jnp.float32
    )
    grad_values = jnp.einsum(
        "chlm,clhd->cmhd",
        soft_probs.astype(jnp.bfloat16),
        grad_mixed,
        preferred_element_type=jnp.float32,
    )
    grad_scores = soft_probs * (
        grad_probs - jnp.sum(grad_probs * soft_probs, axis=-1, keepdims=True)
    )
    grad_low = grad_scores.astype(jnp.bfloat16)
    grad_queries = (
        jnp.einsum("chlm,cmhd->clhd", grad_low, keys_in, preferred_element_type=jnp.float32)
        * score_scale
    )
    grad_keys = (
        jnp.einsum("chlm,clhd->cmhd", grad_low, queries, preferred_element_type=jnp.float32)
        * score_scale
    )
    return jnp.stack([grad_queries, grad_keys, grad_values], axis=2)


def adam_update(gradient, first_moment, second_moment):
    first_new = decay_first * first_moment + (1.0 - decay_first) * gradient
    second_new = decay_second * second_moment + (1.0 - decay_second) * gradient * gradient
    step_dir = first_new / correct_first / (jnp.sqrt(second_new / correct_second) + adam_epsilon)
    return (step_dir, first_new)


def per_device(
    tokens,
    cotangent,
    deletion,
    lengths,
    qkv_weight,
    out_weight,
    up_weight,
    down_weight,
    vectors,
    qkv_first,
    out_first,
    up_first,
    down_first,
    vector_first,
    qkv_second,
    out_second,
    up_second,
    down_second,
    vector_second,
):
    crop_count = lengths.shape[0]
    head_size = D // H
    qkv_low = qkv_weight.astype(jnp.bfloat16)
    out_low = out_weight.astype(jnp.bfloat16)
    up_low = up_weight.astype(jnp.bfloat16)
    down_low = down_weight.astype(jnp.bfloat16)
    vector_low = vectors.astype(jnp.bfloat16)
    gathered = (
        lax.all_gather(qkv_low, "shard", axis=0, tiled=True),
        lax.all_gather(out_low, "shard", axis=0, tiled=True),
        lax.all_gather(up_low, "shard", axis=0, tiled=True),
        lax.all_gather(down_low, "shard", axis=0, tiled=True),
        lax.all_gather(vector_low, "shard", axis=1, tiled=True),
    )
    qkv_full, out_full, up_full, down_full, vector_full = gathered
    vector_float = vector_full.astype(jnp.float32)
    places = jnp.arange(CROP, dtype=jnp.int32)[None, :]
    allowed = ((deletion == 1) | (places == 0)) & (places < lengths[:, None])
    block_crops = math.gcd(crop_count, max(1, 512 // CROP))
    block_count = crop_count // block_crops
    allowed_blocks = allowed.reshape(block_count, block_crops, CROP)
    qkv_bias = jnp.concatenate([vector_float[0], jnp.zeros((D,), jnp.float32), vector_float[1]])
    qkv_act = (jnp.dot(tokens, qkv_full, preferred_element_type=jnp.float32) + qkv_bias).astype(
        jnp.bfloat16
    )
    packed = qkv_act.reshape(block_count, block_crops, CROP, 3, H, head_size)
    mixed_rows, log_totals = lax.map(attend_block, (packed, allowed_blocks))
    mixed_low = mixed_rows.reshape(crop_count * CROP, D).astype(jnp.bfloat16)
    branch = jnp.dot(mixed_low, out_full, preferred_element_type=jnp.float32) + vector_float[2]
    first_out, first_normed, first_root = layer_norm(
        tokens.astype(jnp.float32) + branch, vector_float[3], vector_float[4]
    )
    first_low = first_out.astype(jnp.bfloat16)
    inner_act = jnp.dot(first_low, up_full, preferred_element_type=jnp.float32) + vector_float[
        5:9
    ].reshape(FF)
    activated, gelu_back = jax.vjp(partial(jax.nn.gelu, approximate=False), inner_act)
    act_low = activated.astype(jnp.bfloat16)
    second = jnp.dot(act_low, down_full, preferred_element_type=jnp.float32) + vector_float[9]
    result, second_normed, second_root = layer_norm(
        first_out + second, vector_float[10], vector_float[11]
    )
    output = result.astype(jnp.bfloat16)
    back_set = (
        lax.all_gather(qkv_low, "shard", axis=0, tiled=True),
        lax.all_gather(out_low, "shard", axis=0, tiled=True),
        lax.all_gather(up_low, "shard", axis=0, tiled=True),
        lax.all_gather(down_low, "shard", axis=0, tiled=True),
        lax.all_gather(vector_low, "shard", axis=1, tiled=True),
    )
    qkv_back, out_back, up_back, down_back, vector_back = back_set
    vector_again = vector_back.astype(jnp.float32)
    keep_rows = allowed.reshape(crop_count * CROP).astype(jnp.float32)
    grad_result = cotangent.astype(jnp.float32) * keep_rows[:, None]
    grad_sum2, second_gain_grad, second_shift_grad = norm_back(
        grad_result, second_normed, second_root, vector_again[10]
    )
    grad_second = grad_sum2.astype(jnp.bfloat16)
    down_bias_grad = jnp.sum(grad_second, axis=0, dtype=jnp.float32)
    grad_down = jnp.einsum("tf,td->fd", act_low, grad_second, preferred_element_type=jnp.float32)
    grad_act = jnp.einsum("td,fd->tf", grad_second, down_back, preferred_element_type=jnp.float32)
    grad_inner = gelu_back(grad_act)[0].astype(jnp.bfloat16)
    up_bias_grad = jnp.sum(grad_inner, axis=0, dtype=jnp.float32)
    grad_up = jnp.einsum("td,tf->df", first_low, grad_inner, preferred_element_type=jnp.float32)
    grad_first = grad_sum2 + jnp.einsum(
        "tf,df->td", grad_inner, up_back, preferred_element_type=jnp.float32
    )
    grad_sum1, first_gain_grad, first_shift_grad = norm_back(
        grad_first, first_normed, first_root, vector_again[3]
    )
    grad_branch = grad_sum1.astype(jnp.bfloat16)
    out_bias_grad = jnp.sum(grad_branch, axis=0, dtype=jnp.float32)
    grad_out = jnp.einsum("td,te->de", mixed_low, grad_branch, preferred_element_type=jnp.float32)
    grad_mixed = jnp.einsum(
        "te,de->td", grad_branch, out_back, preferred_element_type=jnp.float32
    ).astype(jnp.bfloat16)
    grad_blocks = grad_mixed.reshape(block_count, block_crops, CROP, H, head_size)
    grad_packed = lax.map(attend_back, (packed, allowed_blocks, log_totals, grad_blocks))
    grad_qkv = grad_packed.reshape(crop_count * CROP, 3 * D).astype(jnp.bfloat16)
    bias_sums = jnp.sum(grad_qkv, axis=0, dtype=jnp.float32)
    grad_qkv_weight = jnp.einsum("td,te->de", tokens, grad_qkv, preferred_element_type=jnp.float32)
    token_grad = (
        grad_sum1 + jnp.einsum("te,de->td", grad_qkv, qkv_back, preferred_element_type=jnp.float32)
    ).astype(jnp.bfloat16)
    grad_vectors = jnp.concatenate(
        [
            jnp.stack(
                [
                    bias_sums[:D],
                    bias_sums[2 * D :],
                    out_bias_grad,
                    first_gain_grad,
                    first_shift_grad,
                ]
            ),
            up_bias_grad.reshape(4, D),
            jnp.stack([down_bias_grad, second_gain_grad, second_shift_grad]),
        ],
        axis=0,
    )
    group_sums = (
        lax.psum_scatter(grad_qkv_weight, "shard", scatter_dimension=0, tiled=True),
        lax.psum_scatter(grad_out, "shard", scatter_dimension=0, tiled=True),
        lax.psum_scatter(grad_up, "shard", scatter_dimension=0, tiled=True),
        lax.psum_scatter(grad_down, "shard", scatter_dimension=0, tiled=True),
        lax.psum_scatter(grad_vectors, "shard", scatter_dimension=1, tiled=True),
    )
    gradients = (
        lax.psum(group_sums[0].astype(jnp.bfloat16), "rep").astype(jnp.float32),
        lax.psum(group_sums[1].astype(jnp.bfloat16), "rep").astype(jnp.float32),
        lax.psum(group_sums[2].astype(jnp.bfloat16), "rep").astype(jnp.float32),
        lax.psum(group_sums[3].astype(jnp.bfloat16), "rep").astype(jnp.float32),
        lax.psum(group_sums[4].astype(jnp.bfloat16), "rep").astype(jnp.float32),
    )
    firsts = (qkv_first, out_first, up_first, down_first, vector_first)
    seconds = (qkv_second, out_second, up_second, down_second, vector_second)
    updated = [
        adam_update(gradient, first_moment, second_moment)
        for gradient, first_moment, second_moment in zip(gradients, firsts, seconds)
    ]
    return (
        output,
        token_grad,
        gradients[0],
        gradients[1],
        gradients[2],
        gradients[3],
        gradients[4],
        updated[0][0],
        updated[1][0],
        updated[2][0],
        updated[3][0],
        updated[4][0],
        updated[0][1],
        updated[1][1],
        updated[2][1],
        updated[3][1],
        updated[4][1],
    )


def solution(mesh):
    placed = (
        P(("rep", "shard"), None),
        P(("rep", "shard"), None),
        P(("rep", "shard"), None),
        P(("rep", "shard")),
        P("shard", None),
        P("shard", None),
        P("shard", None),
        P("shard", None),
        P(None, "shard"),
        P("shard", None),
        P("shard", None),
        P("shard", None),
        P("shard", None),
        P(None, "shard"),
        P("shard", None),
        P("shard", None),
        P("shard", None),
        P("shard", None),
        P(None, "shard"),
    )
    return jax.shard_map(
        per_device,
        mesh=mesh,
        in_specs=placed,
        out_specs=(
            P(("rep", "shard"), None),
            P(("rep", "shard"), None),
            P("shard", None),
            P("shard", None),
            P("shard", None),
            P("shard", None),
            P(None, "shard"),
            P("shard", None),
            P("shard", None),
            P("shard", None),
            P("shard", None),
            P(None, "shard"),
            P("shard", None),
            P("shard", None),
            P("shard", None),
            P("shard", None),
            P(None, "shard"),
        ),
        check_vma=False,
    )
```

profile of v0, /device:TPU:0, one launch (start us, length us, event | category | flops | bytes accessed | tf_op | source)
XLA Modules:
  0.0 704.1 jit_solution(15059409197622101852)
XLA Ops:
  14.6 15.8 %all-gather = bf16[8,96,12]{1,2,0:T(8,128)(2,1)S(1)} all-gather(bf16[1,96,12]{1,2,0:T(8,128)(2,1)S(1)} %convert_bitcast_fusion.1), channel_id=1, replica_groups=mesh['rep'=4,'shard'=8] {'shard'}, dimensions={0}, use_global_device_ids=true | all-gather | bytes 20736 | tf_op jit(solution)/shard_map/all_gather | solution.py:135
  35.1 19.5 %all-gather.6.cloned.1.call-done = bf16[768,2304]{1,0:T(8,128)(2,1)} async-done(((bf16[96,2304]{1,0:T(8,128)(2,1)}), bf16[768,2304]{1,0:T(8,128)(2,1)}) %all-gather.6.cloned.1.call-update) | async-done | bytes 3538960 | tf_op jit(solution)/shard_map/all_gather | solution.py:131
  68.8 8.9 %reshape.144 = bf16[2,2,256,3,12,64]{2,1,0,5,4,3:T(2,128)(2,1)} reshape(bf16[1024,2304]{0,1:T(8,128)(2,1)} %copy.109) | data formatting | bytes 9437184 | tf_op jit(solution)/shard_map/reshape | solution.py:148
  83.2 12.7 %while.22 = (s32[]{:T(128)}, bf16[2,2,256,12,64]{2,4,3,1,0:T(8,128)(2,1)S(1)}, f32[2,2,12,256]{3,2,1,0:T(8,128)S(1)}, bf16[2,2,256,3,12,64]{2,5,4,1,3,0:T(8,128)...) while((s32[]{:T(128)}, bf16[2,2,256,12,64]{2,4,3,1,0:T(8,128)(2,1)S(1)}, f32[2,2,12,256]{3,2,1,0:T(8,128)S(1)}, ...), condition=%wide.region_3.4_spmd, body=%wide.region_0.3_spmd.sunk | while | flops 419948544 | bytes 27766356 | solution.py:149
  104.1 28.0 %all-gather.10.cloned.1.call-done = bf16[768,3072]{1,0:T(8,128)(2,1)} async-done(((bf16[96,3072]{1,0:T(8,128)(2,1)}), bf16[768,3072]{1,0:T(8,128)(2,1)}) %all-gather.10.cloned.1.call-update) | async-done | bytes 4718608 | tf_op jit(solution)/shard_map/all_gather | solution.py:133
  132.2 37.8 %multiply_convert_fusion.1 = (bf16[1024,3072]{1,0:T(8,128)(2,1)}, f32[1024,3072]{1,0:T(8,128)}, f32[1024,3072]{1,0:T(8,128)}) fusion(f32[3072]{0:T(1024)S(1)} %add.200, bf16[768,3072]{1,0:T(8,128)(2,1)} %all-gather.10.cloned.1.call-done, f32[1024,768]{0,1:T(8,128)S(1)} %get-tuple-element.266, f32[768]{0:T(1024)S(1)} %get-tuple-element.203, ...), kind=kOutput, calls=%fused_computation.50 | convolution fusion | flops 5043388416 | bytes 39348224 | tf_op jit(solution)/shard_map/dot_general | solution.py:156
  169.9 14.8 %all-gather.12.cloned.1.call-done = bf16[3072,768]{1,0:T(8,128)(2,1)} async-done(((bf16[384,768]{1,0:T(8,128)(2,1)}), bf16[3072,768]{1,0:T(8,128)(2,1)}) %all-gather.12.cloned.1.call-update) | async-done | bytes 4718608 | tf_op jit(solution)/shard_map/all_gather | solution.py:134
  184.8 9.4 %fusion.73 = (f32[1024]{0:T(1024)S(1)}, f32[1024,768]{0,1:T(8,128)S(1)}) fusion(f32[768]{0:T(1024)S(1)} %copy-done.39, bf16[1024,3072]{1,0:T(8,128)(2,1)} %get-tuple-element.254, bf16[3072,768]{1,0:T(8,128)(2,1)} %all-gather.12.cloned.1.call-done, f32[768]{0:T(1024)S(1)} %get-tuple-element.203, f32[768]{0:T(1024)S(1)} %get-tuple-element.204, ...), kind=kOutput, calls=%fused_computation.158 | convolution fusion | flops 4837342208 | bytes 17323008 | tf_op jit(solution)/shard_map/dot_general | solution.py:161
  201.0 18.1 %convert_reduce_fusion = (f32[3072]{0:T(1024)}, bf16[1024,3072]{1,0:T(8,128)(2,1)}) fusion(f32[1024,3072]{1,0:T(8,128)} %get-tuple-element.255, bf16[1024,768]{0,1:T(8,128)(2,1)S(1)} %get-tuple-element.249, bf16[3072,768]{1,0:T(8,128)(2,1)} %all-gather.12.cloned.1.call-done, f32[1024,3072]{1,0:T(8,128)} %get-tuple-element.267, f32[3072]{0:T(1024)S(1)} %add.200), kind=kOutput, calls=%fused_computation.48 | convolution fusion | flops 4885312512 | bytes 37773312 | tf_op jit(solution)/shard_map/td,fd->tf/dot_general | solution.py:183
  219.1 11.2 %multiply_reduce_fusion.2 = (f32[768]{0:T(1024)S(1)}, f32[1024]{0:T(1024)S(1)}, f32[1024]{0:T(1024)S(1)}, f32[768]{0:T(1024)S(1)}, f32[1024,768]{0,1:T(8,128)S(1)}) fusion(f32[1024,768]{0,1:T(8,128)} %copy-done.1, f32[1024]{0:T(1024)S(1)} %add_rsqrt_fusion.1, f32[1024]{0:T(1024)S(1)} %broadcast_multiply_fusion.5, f32[768]{0:T(1024)S(1)} %get-tuple-element.204, ...), kind=kOutput, calls=%fused_computation.69 | convolution fusion | flops 4846776320 | bytes 22069248 | tf_op jit(solution)/shard_map/tf,df->td/dot_general | solution.py:187
  241.4 25.9 %while.23 = (s32[]{:T(128)}, bf16[2,2,256,3,12,64]{2,5,4,1,3,0:T(8,128)(2,1)}, bf16[2,2,256,3,12,64]{2,5,4,1,3,0:T(8,128)(2,1)}, pred[2,2,256]{2,1,0:T(4,128)(4,...) while((s32[]{:T(128)}, ...), condition=%wide.region_14.15_spmd, body=%wide.region_12.14_spmd.sunk | while | flops 1038870528 | bytes 66244188 | solution.py:200
  267.3 9.4 %copy.118 = bf16[2,2,256,3,12,64]{2,1,0,5,4,3:T(2,128)(2,1)} copy(bf16[2,2,256,3,12,64]{2,5,4,1,3,0:T(8,128)(2,1)} %get-tuple-element.79) | data formatting | bytes 9437184 | tf_op jit(solution)/shard_map/convert_element_type | solution.py:201
  276.7 8.8 %convert_element_type.148 = bf16[1024,2304]{0,1:T(8,128)(2,1)} reshape(bf16[2,2,256,3,12,64]{2,1,0,5,4,3:T(2,128)(2,1)} %copy.118) | data formatting | bytes 9437184 | tf_op jit(solution)/shard_map/convert_element_type | solution.py:201
  285.6 8.3 %convolution_bitcast_fusion = f32[768,2304]{0,1:T(8,128)} fusion(bf16[1024,2304]{0,1:T(8,128)(2,1)} %convert_element_type.148, bf16[1024,768]{1,0:T(8,128)(2,1)S(1)} %copy-done.8), kind=kOutput, calls=%fused_computation.66 | convolution fusion | flops 3623878656 | bytes 13369344 | tf_op jit(solution)/shard_map/td,te->de/dot_general | solution.py:203
  293.9 8.0 %copy.134 = f32[768,2304]{1,0:T(8,128)} copy(f32[768,2304]{0,1:T(8,128)} %convolution_bitcast_fusion) | data formatting | bytes 14155776
  303.3 10.1 %fusion.74 = f32[3072,768]{1,0:T(8,128)} fusion(bf16[1024,3072]{1,0:T(8,128)(2,1)} %get-tuple-element.254, bf16[1024,768]{0,1:T(8,128)(2,1)S(1)} %copy-done.12), kind=kOutput, calls=%fused_computation.159 | convolution fusion | flops 4831838208 | bytes 17301504 | tf_op jit(solution)/shard_map/tf,td->fd/dot_general | solution.py:182
  315.4 10.5 %fusion.64 = f32[768,3072]{1,0:T(8,128)} fusion(bf16[1024,3072]{1,0:T(8,128)(2,1)} %get-tuple-element.272, f32[1024,768]{0,1:T(8,128)S(1)} %copy-done.3, f32[768]{0:T(1024)S(1)} %copy-done.38, f32[768]{0:T(1024)S(1)} %get-tuple-element.204, f32[1024]{0:T(1024)S(1)} %add_rsqrt_fusion.1, f32[1024]{0:T(1024)S(1)} %broadcast_multiply_fusion.5), kind=kOutput, calls=%fused_computation.154 | convolution fusion | flops 4835770368 | bytes 18888704 | tf_op jit(solution)/shard_map/td,tf->df/dot_general | solution.py:186
  332.2 45.9 %reduce-scatter.16.cloned.1.call-done = f32[96,2304]{1,0:T(8,128)} async-done(((f32[768,2304]{1,0:T(8,128)}), f32[96,2304]{1,0:T(8,128)}) %reduce-scatter.16.cloned.1.call-update) | async-done | bytes 884752
  380.3 98.0 %reduce-scatter.14.cloned.1.call-done = f32[384,768]{1,0:T(8,128)} async-done(((f32[3072,768]{1,0:T(8,128)}), f32[384,768]{1,0:T(8,128)}) %reduce-scatter.14.cloned.1.call-update) | async-done | bytes 1179664 | tf_op jit(solution)/shard_map/reduce_scatter | solution.py:227
  480.4 98.1 %reduce-scatter.12.cloned.1.call-done = f32[96,3072]{1,0:T(8,128)} async-done(((f32[768,3072]{1,0:T(8,128)}), f32[96,3072]{1,0:T(8,128)}) %reduce-scatter.12.cloned.1.call-update) | async-done | bytes 1179664 | tf_op jit(solution)/shard_map/reduce_scatter | solution.py:226
  583.6 9.3 %add_convert_fusion.2 = bf16[1024,768]{0,1:T(8,128)(2,1)} fusion(f32[1024,768]{0,1:T(8,128)} %copy-done.5, bf16[768,2304]{1,0:T(8,128)(2,1)} %all-gather.6.cloned.1.call-done, bf16[1024,2304]{0,1:T(8,128)(2,1)} %convert_element_type.148), kind=kOutput, calls=%fused_computation.71 | convolution fusion | flops 3625451520 | bytes 12976128 | tf_op jit(solution)/shard_map/te,de->td/dot_general | solution.py:205
  597.2 13.2 %reduce-scatter.18.cloned.1.call-done = f32[96,12]{1,0:T(8,128)} async-done(((f32[768,12]{1,0:T(8,128)}), f32[96,12]{1,0:T(8,128)}) %reduce-scatter.18.cloned.1.call-update) | async-done | bytes 4624
  611.3 10.2 %psum.39 = bf16[12,96]{1,0:T(8,128)(2,1)S(1)} all-reduce(bf16[12,96]{1,0:T(8,128)(2,1)S(1)} %copy.137), channel_id=1, replica_groups=mesh['rep'=4,'shard'=8] {'rep'}, use_global_device_ids=true, to_apply=%region_32.33 | all-reduce | flops 1152 | bytes 4608 | tf_op jit(solution)/shard_map/psum | solution.py:235
  622.1 58.8 %all-reduce.3.cloned.1.call-done = (bf16[96,2304]{0,1:T(8,128)(2,1)}, bf16[96,768]{1,0:T(8,128)(2,1)}, bf16[96,3072]{1,0:T(8,128)(2,1)}, bf16[384,768]{1,0:T(8,128)(2,1)}) async-done(((bf16[96,2304]{0,1:T(8,128)(2,1)}, bf16[96,768]{1,0:T(8,128)(2,1)}, bf16[96,3072]{1,0:T(8,128)(2,1)}, bf16[384,768]{1,0:T(8,128)(2,1)}), (bf16[96,2304]{0,1:T(8,128)(2,1)}, bf16[96,768]{1,0:T(8,128)(2,1)}, ...) | async-done | bytes 1769488 | tf_op jit(solution)/shard_map/psum | solution.py:231
  (213 shorter events, 136.3 us)
Async XLA Ops:
  7.2 47.4 %all-gather.6.cloned.1.call-start = ((), (), s32[]{:S(2)}) async-start(), calls=%async_computation.5 | async-start | bytes 3981312 | tf_op jit(solution)/shard_map/all_gather | solution.py:131
  9.3 21.8 %copy-start.40 = (s32[4,256]{1,0:T(4,128)S(1)}, s32[4,256]{1,0:T(4,128)}, u32[]{:S(2)}) copy-start(s32[4,256]{1,0:T(4,128)} %param.25) | copy-start | bytes 12292
  9.3 21.8 %copy-start.41 = (s32[4]{0:T(128)S(1)}, s32[4]{0:T(128)}, u32[]{:S(2)}) copy-start(s32[4]{0:T(128)} %param.26) | copy-start | bytes 52
  9.3 21.9 %copy-start.7 = (bf16[1024,768]{1,0:T(8,128)(2,1)S(1)}, bf16[1024,768]{1,0:T(8,128)(2,1)}, u32[]{:S(2)}) copy-start(bf16[1024,768]{1,0:T(8,128)(2,1)} %param.23) | copy-start | bytes 4718596
  9.3 90.5 %all-gather.8.cloned.1.call-start = ((), (), s32[]{:S(2)}) async-start(), calls=%async_computation.6 | async-start | bytes 1327104 | tf_op jit(solution)/shard_map/all_gather | solution.py:132
  11.2 121.0 %all-gather.10.cloned.1.call-start = ((), (), s32[]{:S(2)}) async-start(), calls=%async_computation.7 | async-start | bytes 5308416 | tf_op jit(solution)/shard_map/all_gather | solution.py:133
  12.1 21.4 %copy-start.6 = (bf16[1024,768]{1,0:T(8,128)(2,1)S(1)}, bf16[1024,768]{1,0:T(8,128)(2,1)}, u32[]{:S(2)}) copy-start(bf16[1024,768]{1,0:T(8,128)(2,1)} %param.24) | copy-start | bytes 4718596
  12.1 172.7 %all-gather.12.cloned.1.call-start = ((), (), s32[]{:S(2)}) async-start(), calls=%async_computation.8 | async-start | bytes 5308416 | tf_op jit(solution)/shard_map/all_gather | solution.py:134
  14.5 316.1 %reduce-scatter.10.cloned.1.call-start = ((), (), s32[]{:S(2)}) async-start(), calls=%async_computation.9 | async-start | bytes 2654208 | tf_op jit(solution)/shard_map/reduce_scatter | solution.py:225
  31.1 153.7 %copy-start.37 = (f32[768]{0:T(1024)}, f32[768]{0:T(1024)S(1)}, u32[]{:S(2)}) copy-start(f32[768]{0:T(1024)S(1)} %get-tuple-element.203) | copy-start | bytes 9220
  77.7 5.5 copy-start.10
  103.7 81.1 %copy-start.1 = (f32[1024,768]{0,1:T(8,128)}, f32[1024,768]{0,1:T(8,128)S(1)}, u32[]{:S(2)}) copy-start(f32[1024,768]{0,1:T(8,128)S(1)} %get-tuple-element.266) | copy-start | bytes 9437188
  132.2 52.6 %copy-start.39 = (f32[768]{0:T(1024)S(1)}, f32[768]{0:T(1024)}, u32[]{:S(2)}) copy-start(f32[768]{0:T(1024)} %get-tuple-element.202) | copy-start | bytes 9220
  201.0 18.1 %copy-start.11 = (bf16[1024,768]{0,1:T(8,128)(2,1)}, bf16[1024,768]{0,1:T(8,128)(2,1)S(1)}, u32[]{:S(2)}) copy-start(bf16[1024,768]{0,1:T(8,128)(2,1)S(1)} %get-tuple-element.249) | copy-start | bytes 4718596
  219.1 11.2 %copy-start.2 = (f32[1024,768]{0,1:T(8,128)S(1)}, f32[1024,768]{0,1:T(8,128)}, u32[]{:S(2)}) copy-start(f32[1024,768]{0,1:T(8,128)} %copy-done.1) | copy-start | bytes 9437188
  241.4 136.7 %reduce-scatter.16.cloned.1.call-start = ((), (), s32[]{:S(2)}) async-start(), calls=%async_computation.12 | async-start | bytes 7962624
  276.7 8.8 %copy-start.8 = (bf16[1024,768]{1,0:T(8,128)(2,1)S(1)}, bf16[1024,768]{1,0:T(8,128)(2,1)}, u32[]{:S(2)}) copy-start(bf16[1024,768]{1,0:T(8,128)(2,1)} %param.23) | copy-start | bytes 4718596
  301.9 176.4 %reduce-scatter.14.cloned.1.call-start = ((), (), s32[]{:S(2)}) async-start(), calls=%async_computation.11 | async-start | bytes 10616832 | tf_op jit(solution)/shard_map/reduce_scatter | solution.py:227
  313.4 265.1 %reduce-scatter.12.cloned.1.call-start = ((), (), s32[]{:S(2)}) async-start(), calls=%async_computation.10 | async-start | bytes 10616832 | tf_op jit(solution)/shard_map/reduce_scatter | solution.py:226
  326.0 284.4 %reduce-scatter.18.cloned.1.call-start = ((), (), s32[]{:S(2)}) async-start(), calls=%async_computation.13 | async-start | bytes 442368
  330.5 350.4 %all-reduce.3.cloned.1.call-start = ((), (), s32[]{:S(2)}) async-start(), calls=%async_computation.14 | async-start | bytes 3833856 | tf_op jit(solution)/shard_map/psum | solution.py:231
  332.2 248.5 %copy-start.18 = (f32[96,2304]{1,0:T(8,128)S(1)}, f32[96,2304]{1,0:T(8,128)}, u32[]{:S(2)}) copy-start(f32[96,2304]{1,0:T(8,128)} %param.32) | copy-start | bytes 2654212
  593.0 28.5 %copy-start.35 = (f32[12,96]{1,0:T(8,128)S(1)}, f32[12,96]{1,0:T(8,128)}, u32[]{:S(2)}) copy-start(f32[12,96]{1,0:T(8,128)} %param.41) | copy-start | bytes 13828
  593.0 28.5 %copy-start.36 = (f32[12,96]{1,0:T(8,128)S(1)}, f32[12,96]{1,0:T(8,128)}, u32[]{:S(2)}) copy-start(f32[12,96]{1,0:T(8,128)} %param.36) | copy-start | bytes 13828
  (28 other events, 77.2 us)
Sparse Core Ops, SparseCore 0:
  10.2 44.3 all-gather.5
  56.8 21.5 all-gather.7
  80.7 51.4 all-gather.9
  134.2 50.5 all-gather.11
  241.5 35.2 reduce-scatter.9
  302.0 76.0 reduce-scatter.15
  380.4 97.8 reduce-scatter.13
  480.6 97.8 reduce-scatter.11
  581.3 29.0 reduce-scatter.17
  615.3 65.5 all-reduce.2
where the time goes:
time: 715 us; the launch traced here: 704 us
  waiting for transfers between devices  376 us (53%)
  matrix products  152 us (21%)
  local copies, waits for them, and re-layouts  89.8 us (13%)
  other arithmetic  43.7 us (6%)
  blocking collectives  26 us (4%)
  between operations  15.2 us (2%)
    reduce_scatter x1, waiting for transfers between devices, per_device(): lax.psum_scatter(grad_up, 'shard', scatter_dimension=0, tiled=True)  98.1 us
    reduce_scatter x1, waiting for transfers between devices, per_device(): lax.psum_scatter(grad_down, 'shard', scatter_dimension=0, tiled=True)  98 us
    unnamed x12, waiting for transfers between devices  59.3 us
    psum x1, waiting for transfers between devices, per_device(): lax.psum(group_sums[0].astype(jnp.bfloat16), 'rep').astype(jnp.float32)  58.8 us
    dot_general x1, matrix products, per_device(): jnp.dot(first_low, up_full, preferred_element_type=jnp.float32)  37.8 us
    unnamed x98, local copies, waits for them, and re-layouts  33.9 us
    all_gather x1, waiting for transfers between devices, per_device(): lax.all_gather(up_low, 'shard', axis=0, tiled=True)  28 us
    all_gather x1, waiting for transfers between devices, per_device(): lax.all_gather(qkv_low, 'shard', axis=0, tiled=True)  19.5 us
  transfers between devices with their start and end apart: 10, of which 8 were waited for; matrix products, arithmetic and copies ran while one was open for 30% of the time, Pallas kernels for 0%

commit v1 on v0

--- a/solution.py
+++ b/solution.py
@@ -15,6 +15,27 @@
 correct_first = 1.0 - 2.6561398887587544e-05
 correct_second = 0.0952078528862904
 adam_epsilon = 1e-08
+
+
+def collect(value, axis, dim):
+    size, here, span = (lax.axis_size(axis), lax.axis_index(axis), value.shape[dim])
+    forward = [(i, (i + 1) % size) for i in range(size)]
+    left = [(i, (i - 1) % size) for i in range(size)]
+    whole = jnp.zeros((*value.shape[:dim], size * span, *value.shape[dim + 1 :]), value.dtype)
+    whole = lax.dynamic_update_slice_in_dim(whole, value, here * span, axis=dim)
+    from_left = from_right = value
+    halfway = size // 2
+    for step in range(1, halfway + 1):
+        from_left = lax.ppermute(from_left, axis, forward)
+        whole = lax.dynamic_update_slice_in_dim(
+            whole, from_left, (here - step) % size * span, axis=dim
+        )
+        if step < size - halfway:
+            from_right = lax.ppermute(from_right, axis, left)
+            whole = lax.dynamic_update_slice_in_dim(
+                whole, from_right, (here + step) % size * span, axis=dim
+            )
+    return whole
 
 
 def layer_norm(hidden, gain_row, shift_row):
@@ -128,7 +149,7 @@
     down_low = down_weight.astype(jnp.bfloat16)
     vector_low = vectors.astype(jnp.bfloat16)
     gathered = (
-        lax.all_gather(qkv_low, "shard", axis=0, tiled=True),
+        collect(qkv_low, "shard", 0),
         lax.all_gather(out_low, "shard", axis=0, tiled=True),
         lax.all_gather(up_low, "shard", axis=0, tiled=True),
         lax.all_gather(down_low, "shard", axis=0, tiled=True),

time: 715 us -> 767 us (1.073)
  waiting for transfers between devices: 376 us -> 406 us
  starting transfers between devices: 0.41 us -> 12.2 us
  blocking collectives: 26 us -> 35.9 us
    ppermute x0 -> x7, waiting for transfers between devices: none -> 47.2 us  [the longest x4 45.3 us: collect(): from_left = lax.ppermute(from_left, axis, forward)]
    all_gather x1, waiting for transfers between devices: 28 us -> 0.02 us  [per_device(): lax.all_gather(up_low, 'shard', axis=0, tiled=True)]
    all_gather x1, waiting for transfers between devices: 19.5 us -> 37 us  [per_device(): lax.all_gather(qkv_low, 'shard', axis=0, tiled=True)]
    all_gather x1, waiting for transfers between devices: 14.8 us -> 0.01 us  [per_device(): lax.all_gather(down_low, 'shard', axis=0, tiled=True)]
    ppermute x0 -> x7, starting transfers between devices: none -> 11.8 us  [the longest x3 10.8 us: collect(): from_right = lax.ppermute(from_right, axis, left)]
    all_gather x1, blocking collectives: 15.8 us -> 25.6 us  [per_device(): lax.all_gather(vector_low, 'shard', axis=1, tiled=True)]
    unnamed x12, waiting for transfers between devices: 59.3 us -> 67.1 us
    unnamed x98 -> x96, local copies, waits for them, and re-layouts: 33.9 us -> 37.8 us
  transfers between devices with their start and end apart: 10 -> 17, of which waited for: 8 -> 10; matrix products, arithmetic and copies ran while one was open for 30% -> 28% of each run, Pallas kernels for 0% -> 0%
where the time goes in v1:
time: 767 us; the launch traced here: 762 us
  waiting for transfers between devices  406 us (53%)
  matrix products  151 us (20%)
  local copies, waits for them, and re-layouts  93.4 us (12%)
  other arithmetic  47.2 us (6%)
  blocking collectives  35.9 us (5%)
  between operations  15.4 us (2%)
  starting transfers between devices  12.2 us (2%)
    reduce_scatter x1, waiting for transfers between devices, per_device(): lax.psum_scatter(grad_up, 'shard', scatter_dimension=0, tiled=True)  98.1 us
    reduce_scatter x1, waiting for transfers between devices, per_device(): lax.psum_scatter(grad_down, 'shard', scatter_dimension=0, tiled=True)  97.8 us
    unnamed x12, waiting for transfers between devices  67.1 us
    psum x1, waiting for transfers between devices, per_device(): lax.psum(group_sums[0].astype(jnp.bfloat16), 'rep').astype(jnp.float32)  58.8 us
    ppermute x4, waiting for transfers between devices, collect(): from_left = lax.ppermute(from_left, axis, forward)  45.3 us
    dot_general x1, matrix products, per_device(): jnp.dot(first_low, up_full, preferred_element_type=jnp.float32)  38.1 us
    unnamed x96, local copies, waits for them, and re-layouts  37.8 us
    all_gather x1, waiting for transfers between devices, per_device(): lax.all_gather(qkv_low, 'shard', axis=0, tiled=True)  37 us
  transfers between devices with their start and end apart: 17, of which 10 were waited for; matrix products, arithmetic and copies ran while one was open for 28% of the time, Pallas kernels for 0%

profile of v1, /device:TPU:0, one launch (start us, length us, event | category | flops | bytes accessed | tf_op | source)
XLA Modules:
  0.0 761.7 jit_solution(12635229544237813118)
XLA Ops:
  20.5 25.6 %all-gather = bf16[8,96,12]{1,2,0:T(8,128)(2,1)S(1)} all-gather(bf16[1,96,12]{1,2,0:T(8,128)(2,1)S(1)} %convert_bitcast_fusion.1), channel_id=1, replica_groups=mesh['rep'=4,'shard'=8] {'shard'}, dimensions={0}, use_global_device_ids=true | all-gather | bytes 20736 | tf_op jit(solution)/shard_map/all_gather | solution.py:156
  65.0 17.8 %collective-permute-done.2 = bf16[96,2304]{1,0:T(8,128)(2,1)S(1)} collective-permute-done((bf16[96,2304]{1,0:T(8,128)(2,1)}, bf16[96,2304]{1,0:T(8,128)(2,1)S(1)}, u32[]{:S(2)}, u32[]{:S(2)}) %collective-permute-start.2) | collective-permute-done | bytes 442400 | tf_op jit(solution)/shard_map/ppermute | solution.py:29
  86.5 16.8 %collective-permute-done.4 = bf16[96,2304]{1,0:T(8,128)(2,1)S(1)} collective-permute-done((bf16[96,2304]{1,0:T(8,128)(2,1)S(1)}, bf16[96,2304]{1,0:T(8,128)(2,1)S(1)}, u32[]{:S(2)}, u32[]{:S(2)}) %collective-permute-start.4) | collective-permute-done | bytes 442400 | tf_op jit(solution)/shard_map/ppermute | solution.py:29
  105.4 10.7 %collective-permute-done.6 = bf16[96,2304]{1,0:T(8,128)(2,1)S(1)} collective-permute-done((bf16[96,2304]{1,0:T(8,128)(2,1)S(1)}, bf16[96,2304]{1,0:T(8,128)(2,1)S(1)}, u32[]{:S(2)}, u32[]{:S(2)}) %collective-permute-start.6) | collective-permute-done | bytes 442400 | tf_op jit(solution)/shard_map/ppermute | solution.py:29
  122.4 8.9 %reshape.144 = bf16[2,2,256,3,12,64]{2,1,0,5,4,3:T(2,128)(2,1)} reshape(bf16[1024,2304]{0,1:T(8,128)(2,1)} %fusion.30) | data formatting | bytes 9437184 | tf_op jit(solution)/shard_map/reshape | solution.py:169
  136.7 13.9 %while.22 = (s32[]{:T(128)}, bf16[2,2,256,12,64]{2,4,3,1,0:T(8,128)(2,1)S(1)}, f32[2,2,12,256]{3,2,1,0:T(8,128)}, bf16[2,2,256,3,12,64]{2,5,4,1,3,0:T(8,128)(2,1)}, pred[2,2,256]{2,1,0:T(4,128)(4,1)S(1)}, /*index=5*/s32[]{:T(128)}) while((s32[]{:T(128)}, bf16[2,2,256,12,64]{2,4,3,1,0:T(8,128)(2,1)S(1)}, f32[2,2,12,256]{3,2,1,0:T(8,128)}, ...), condition=%wide.region_3.4_spmd, body=%wide.region_0.3_spmd.sunk | while | flops 419948544 | bytes 27742288 | solution.py:170
  159.3 38.1 %multiply_convert_fusion.1 = (bf16[1024,3072]{1,0:T(8,128)(2,1)}, f32[1024,3072]{1,0:T(8,128)}, f32[1024,3072]{1,0:T(8,128)}) fusion(f32[3072]{0:T(1024)S(1)} %copy-done.31, bf16[768,3072]{1,0:T(8,128)(2,1)} %all-gather.8.cloned.1.call-done, f32[1024,768]{0,1:T(8,128)S(1)} %get-tuple-element.268, f32[768]{0:T(1024)S(1)} %get-tuple-element.203, ...), kind=kOutput, calls=%fused_computation.50 | convolution fusion | flops 5043388416 | bytes 39348224 | tf_op jit(solution)/shard_map/dot_general | solution.py:177
  197.4 9.4 %fusion.74 = (f32[1024]{0:T(1024)S(1)}, f32[1024,768]{0,1:T(8,128)S(1)}) fusion(f32[768]{0:T(1024)S(1)} %get-tuple-element.202, bf16[1024,3072]{1,0:T(8,128)(2,1)} %get-tuple-element.254, bf16[3072,768]{1,0:T(8,128)(2,1)} %all-gather.10.cloned.1.call-done, f32[768]{0:T(1024)S(1)} %get-tuple-element.203, f32[768]{0:T(1024)S(1)} %get-tuple-element.204, ...), kind=kOutput, calls=%fused_computation.167 | convolution fusion | flops 4837342208 | bytes 17323008 | tf_op jit(solution)/shard_map/dot_general | solution.py:182
  213.6 18.1 %convert_reduce_fusion = (f32[3072]{0:T(1024)}, bf16[1024,3072]{1,0:T(8,128)(2,1)}) fusion(f32[1024,3072]{1,0:T(8,128)} %get-tuple-element.255, bf16[1024,768]{0,1:T(8,128)(2,1)S(1)} %get-tuple-element.249, bf16[3072,768]{1,0:T(8,128)(2,1)} %all-gather.10.cloned.1.call-done, f32[1024,3072]{1,0:T(8,128)} %get-tuple-element.269, f32[3072]{0:T(1024)S(1)} %copy-done.31), kind=kOutput, calls=%fused_computation.48 | convolution fusion | flops 4885312512 | bytes 37773312 | tf_op jit(solution)/shard_map/td,fd->tf/dot_general | solution.py:204
  231.7 11.2 %multiply_reduce_fusion.2 = (f32[768]{0:T(1024)S(1)}, f32[1024]{0:T(1024)S(1)}, f32[1024]{0:T(1024)S(1)}, f32[768]{0:T(1024)S(1)}, f32[1024,768]{0,1:T(8,128)S(1)}) fusion(f32[1024,768]{0,1:T(8,128)} %copy-done.1, f32[1024]{0:T(1024)S(1)} %add_rsqrt_fusion.1, f32[1024]{0:T(1024)S(1)} %broadcast_multiply_fusion.5, f32[768]{0:T(1024)S(1)} %get-tuple-element.204, ...), kind=kOutput, calls=%fused_computation.70 | convolution fusion | flops 4846776320 | bytes 22069248 | tf_op jit(solution)/shard_map/tf,df->td/dot_general | solution.py:208
  254.1 25.9 %while.23 = (s32[]{:T(128)}, bf16[2,2,256,3,12,64]{2,5,4,1,3,0:T(8,128)(2,1)}, bf16[2,2,256,3,12,64]{2,5,4,1,3,0:T(8,128)(2,1)}, pred[2,2,256]{2,1,0:T(4,128)(4,...) while((s32[]{:T(128)}, ...), condition=%wide.region_14.15_spmd, body=%wide.region_12.14_spmd.sunk | while | flops 1038870528 | bytes 66244188 | solution.py:221
  280.0 9.4 %copy.115 = bf16[2,2,256,3,12,64]{2,1,0,5,4,3:T(2,128)(2,1)} copy(bf16[2,2,256,3,12,64]{2,5,4,1,3,0:T(8,128)(2,1)} %get-tuple-element.79) | data formatting | bytes 9437184 | tf_op jit(solution)/shard_map/convert_element_type | solution.py:222
  289.4 8.8 %convert_element_type.152 = bf16[1024,2304]{0,1:T(8,128)(2,1)} reshape(bf16[2,2,256,3,12,64]{2,1,0,5,4,3:T(2,128)(2,1)} %copy.115) | data formatting | bytes 9437184 | tf_op jit(solution)/shard_map/convert_element_type | solution.py:222
  298.2 8.4 %convolution_bitcast_fusion = f32[768,2304]{0,1:T(8,128)} fusion(bf16[1024,2304]{0,1:T(8,128)(2,1)} %convert_element_type.152, bf16[1024,768]{1,0:T(8,128)(2,1)S(1)} %copy-done.7), kind=kOutput, calls=%fused_computation.66 | convolution fusion | flops 3623878656 | bytes 13369344 | tf_op jit(solution)/shard_map/td,te->de/dot_general | solution.py:224
  316.0 10.2 %fusion.75 = f32[3072,768]{1,0:T(8,128)} fusion(bf16[1024,3072]{1,0:T(8,128)(2,1)} %get-tuple-element.254, bf16[1024,768]{0,1:T(8,128)(2,1)S(1)} %copy-done.11), kind=kOutput, calls=%fused_computation.168 | convolution fusion | flops 4831838208 | bytes 17301504 | tf_op jit(solution)/shard_map/tf,td->fd/dot_general | solution.py:203
  328.1 10.5 %fusion.65 = f32[768,3072]{1,0:T(8,128)} fusion(bf16[1024,3072]{1,0:T(8,128)(2,1)} %get-tuple-element.274, f32[1024,768]{0,1:T(8,128)S(1)} %copy-done.3, f32[768]{0:T(1024)S(1)} %copy-done.37, f32[768]{0:T(1024)S(1)} %get-tuple-element.204, f32[1024]{0:T(1024)S(1)} %add_rsqrt_fusion.1, f32[1024]{0:T(1024)S(1)} %broadcast_multiply_fusion.5), kind=kOutput, calls=%fused_computation.163 | convolution fusion | flops 4835770368 | bytes 18888704 | tf_op jit(solution)/shard_map/td,tf->df/dot_general | solution.py:207
  345.7 47.4 %reduce-scatter.16.cloned.1.call-done = f32[96,2304]{1,0:T(8,128)} async-done(((f32[768,2304]{1,0:T(8,128)}), f32[96,2304]{1,0:T(8,128)}) %reduce-scatter.16.cloned.1.call-update) | async-done | bytes 884752
  395.4 97.8 %reduce-scatter.14.cloned.1.call-done = f32[384,768]{1,0:T(8,128)} async-done(((f32[3072,768]{1,0:T(8,128)}), f32[384,768]{1,0:T(8,128)}) %reduce-scatter.14.cloned.1.call-update) | async-done | bytes 1179664 | tf_op jit(solution)/shard_map/reduce_scatter | solution.py:248
  495.3 98.1 %reduce-scatter.12.cloned.1.call-done = f32[96,3072]{1,0:T(8,128)} async-done(((f32[768,3072]{1,0:T(8,128)}), f32[96,3072]{1,0:T(8,128)}) %reduce-scatter.12.cloned.1.call-update) | async-done | bytes 1179664 | tf_op jit(solution)/shard_map/reduce_scatter | solution.py:247
  598.5 37.0 %all-gather.12.cloned.1.call-done = bf16[768,2304]{1,0:T(8,128)(2,1)} async-done(((bf16[96,2304]{1,0:T(8,128)(2,1)}), bf16[768,2304]{1,0:T(8,128)(2,1)}) %all-gather.12.cloned.1.call-update) | async-done | bytes 3538960 | tf_op jit(solution)/shard_map/all_gather | solution.py:188
  635.5 9.3 %add_convert_fusion.2 = bf16[1024,768]{0,1:T(8,128)(2,1)} fusion(f32[1024,768]{0,1:T(8,128)} %copy-done.5, bf16[768,2304]{1,0:T(8,128)(2,1)} %all-gather.12.cloned.1.call-done, bf16[1024,2304]{0,1:T(8,128)(2,1)} %convert_element_type.152), kind=kOutput, calls=%fused_computation.72 | convolution fusion | flops 3625451520 | bytes 12976128 | tf_op jit(solution)/shard_map/te,de->td/dot_general | solution.py:226
  649.1 18.8 %reduce-scatter.18.cloned.1.call-done = f32[96,12]{1,0:T(8,128)} async-done(((f32[768,12]{1,0:T(8,128)}), f32[96,12]{1,0:T(8,128)}) %reduce-scatter.18.cloned.1.call-update) | async-done | bytes 4624
  668.8 10.3 %psum.39 = bf16[12,96]{1,0:T(8,128)(2,1)S(1)} all-reduce(bf16[12,96]{1,0:T(8,128)(2,1)S(1)} %copy.134), channel_id=1, replica_groups=mesh['rep'=4,'shard'=8] {'rep'}, use_global_device_ids=true, to_apply=%region_32.33 | all-reduce | flops 1152 | bytes 4608 | tf_op jit(solution)/shard_map/psum | solution.py:256
  679.7 58.8 %all-reduce.3.cloned.1.call-done = (bf16[96,2304]{0,1:T(8,128)(2,1)}, bf16[96,768]{1,0:T(8,128)(2,1)}, bf16[96,3072]{1,0:T(8,128)(2,1)}, bf16[384,768]{1,0:T(8,128)(2,1)}) async-done(((bf16[96,2304]{0,1:T(8,128)(2,1)}, bf16[96,768]{1,0:T(8,128)(2,1)}, bf16[96,3072]{1,0:T(8,128)(2,1)}, bf16[384,768]{1,0:T(8,128)(2,1)}), (bf16[96,2304]{0,1:T(8,128)(2,1)}, bf16[96,768]{1,0:T(8,128)(2,1)}, ...) | async-done | bytes 1769488 | tf_op jit(solution)/shard_map/psum | solution.py:252
  (232 shorter events, 164.5 us)
Async XLA Ops:
  7.2 147.5 %all-gather.6.cloned.1.call-start = ((), (), s32[]{:S(2)}) async-start(), calls=%async_computation.5 | async-start | bytes 1327104 | tf_op jit(solution)/shard_map/all_gather | solution.py:153
  8.9 150.1 %all-gather.8.cloned.1.call-start = ((), (), s32[]{:S(2)}) async-start(), calls=%async_computation.6 | async-start | bytes 5308416 | tf_op jit(solution)/shard_map/all_gather | solution.py:154
  11.1 186.2 %all-gather.10.cloned.1.call-start = ((), (), s32[]{:S(2)}) async-start(), calls=%async_computation.7 | async-start | bytes 5308416 | tf_op jit(solution)/shard_map/all_gather | solution.py:155
  12.4 35.9 %copy-start.39 = (s32[4,256]{1,0:T(4,128)S(1)}, s32[4,256]{1,0:T(4,128)}, u32[]{:S(2)}) copy-start(s32[4,256]{1,0:T(4,128)} %param.25) | copy-start | bytes 12292
  12.4 35.9 %copy-start.40 = (s32[4]{0:T(128)S(1)}, s32[4]{0:T(128)}, u32[]{:S(2)}) copy-start(s32[4]{0:T(128)} %param.26) | copy-start | bytes 52
  13.2 46.2 %collective-permute-start = (bf16[96,2304]{1,0:T(8,128)(2,1)}, bf16[96,2304]{1,0:T(8,128)(2,1)}, u32[]{:S(2)}, u32[]{:S(2)}) collective-permute-start(bf16[96,2304]{1,0:T(8,128)(2,1)} %get-tuple-element.257), channel_id=1, source_target_pairs={{0,1},{1,2},{2,3},{3,4},{4,5},{5,6},{6,7},{7,0},{8,9},{9,10},{10,1... | collective-permute-start | bytes 1327112 | tf_op jit(solution)/shard_map/ppermute | solution.py:29
  13.6 46.0 %collective-permute-start.1 = (bf16[96,2304]{1,0:T(8,128)(2,1)}, bf16[96,2304]{1,0:T(8,128)(2,1)}, u32[]{:S(2)}, u32[]{:S(2)}) collective-permute-start(bf16[96,2304]{1,0:T(8,128)(2,1)} %get-tuple-element.257), channel_id=1, source_target_pairs={{0,7},{1,0},{2,1},{3,2},{4,3},{5,4},{6,5},{7,6},{8,15},{9,8},{10,9... | collective-permute-start | bytes 1327112 | tf_op jit(solution)/shard_map/ppermute | solution.py:34
  19.8 324.3 %reduce-scatter.10.cloned.1.call-start = ((), (), s32[]{:S(2)}) async-start(), calls=%async_computation.9 | async-start | bytes 2654208 | tf_op jit(solution)/shard_map/reduce_scatter | solution.py:246
  57.7 58.5 %copy-start.6 = (bf16[1024,768]{1,0:T(8,128)(2,1)S(1)}, bf16[1024,768]{1,0:T(8,128)(2,1)}, u32[]{:S(2)}) copy-start(bf16[1024,768]{1,0:T(8,128)(2,1)} %param.23) | copy-start | bytes 4718596
  59.3 138.1 %copy-start.36 = (f32[768]{0:T(1024)}, f32[768]{0:T(1024)S(1)}, u32[]{:S(2)}) copy-start(f32[768]{0:T(1024)S(1)} %get-tuple-element.203) | copy-start | bytes 9220
  59.3 23.5 %collective-permute-start.2 = (bf16[96,2304]{1,0:T(8,128)(2,1)}, bf16[96,2304]{1,0:T(8,128)(2,1)S(1)}, u32[]{:S(2)}, u32[]{:S(2)}) collective-permute-start(bf16[96,2304]{1,0:T(8,128)(2,1)} %collective-permute-done), channel_id=1, source_target_pairs={{0,1},{1,2},{2,3},{3,4},{4,5},{5,6},{6,7},{7,0},{8,9},{9,10},{10,1... | collective-permute-start | bytes 1327112 | tf_op jit(solution)/shard_map/ppermute | solution.py:29
  59.7 23.2 %collective-permute-start.3 = (bf16[96,2304]{1,0:T(8,128)(2,1)}, bf16[96,2304]{1,0:T(8,128)(2,1)S(1)}, u32[]{:S(2)}, u32[]{:S(2)}) collective-permute-start(bf16[96,2304]{1,0:T(8,128)(2,1)} %collective-permute-done.1), channel_id=1, source_target_pairs={{0,7},{1,0},{2,1},{3,2},{4,3},{5,4},{6,5},{7,6},{8,15},{9,8},{10,9... | collective-permute-start | bytes 1327112 | tf_op jit(solution)/shard_map/ppermute | solution.py:34
  82.9 20.4 %collective-permute-start.4 = (bf16[96,2304]{1,0:T(8,128)(2,1)S(1)}, bf16[96,2304]{1,0:T(8,128)(2,1)S(1)}, u32[]{:S(2)}, u32[]{:S(2)}) collective-permute-start(bf16[96,2304]{1,0:T(8,128)(2,1)S(1)} %collective-permute-done.2), channel_id=1, source_target_pairs={{0,1},{1,2},{2,3},{3,4},{4,5},{5,6},{6,7},{7,0},{8,9},{9,10},{10,1... | collective-permute-start | bytes 1327112 | tf_op jit(solution)/shard_map/ppermute | solution.py:29
  82.9 22.5 %collective-permute-start.5 = (bf16[96,2304]{1,0:T(8,128)(2,1)S(1)}, bf16[96,2304]{1,0:T(8,128)(2,1)S(1)}, u32[]{:S(2)}, u32[]{:S(2)}) collective-permute-start(bf16[96,2304]{1,0:T(8,128)(2,1)S(1)} %collective-permute-done.3), channel_id=1, source_target_pairs={{0,7},{1,0},{2,1},{3,2},{4,3},{5,4},{6,5},{7,6},{8,15},{9,8},{10,9... | collective-permute-start | bytes 1327112 | tf_op jit(solution)/shard_map/ppermute | solution.py:34
  103.3 12.9 %collective-permute-start.6 = (bf16[96,2304]{1,0:T(8,128)(2,1)S(1)}, bf16[96,2304]{1,0:T(8,128)(2,1)S(1)}, u32[]{:S(2)}, u32[]{:S(2)}) collective-permute-start(bf16[96,2304]{1,0:T(8,128)(2,1)S(1)} %collective-permute-done.4), channel_id=1, source_target_pairs={{0,1},{1,2},{2,3},{3,4},{4,5},{5,6},{6,7},{7,0},{8,9},{9,10},{10,1... | collective-permute-start | bytes 1327112 | tf_op jit(solution)/shard_map/ppermute | solution.py:29
  158.5 38.8 %copy-start.1 = (f32[1024,768]{0,1:T(8,128)}, f32[1024,768]{0,1:T(8,128)S(1)}, u32[]{:S(2)}) copy-start(f32[1024,768]{0,1:T(8,128)S(1)} %get-tuple-element.268) | copy-start | bytes 9437188
  254.0 139.1 %reduce-scatter.16.cloned.1.call-start = ((), (), s32[]{:S(2)}) async-start(), calls=%async_computation.12 | async-start | bytes 7962624
  314.6 178.6 %reduce-scatter.14.cloned.1.call-start = ((), (), s32[]{:S(2)}) async-start(), calls=%async_computation.11 | async-start | bytes 10616832 | tf_op jit(solution)/shard_map/reduce_scatter | solution.py:248
  326.2 267.2 %reduce-scatter.12.cloned.1.call-start = ((), (), s32[]{:S(2)}) async-start(), calls=%async_computation.10 | async-start | bytes 10616832 | tf_op jit(solution)/shard_map/reduce_scatter | solution.py:247
  338.7 296.8 %all-gather.12.cloned.1.call-start = ((), (), s32[]{:S(2)}) async-start(), calls=%async_computation.8 | async-start | bytes 3981312 | tf_op jit(solution)/shard_map/all_gather | solution.py:188
  339.5 328.5 %reduce-scatter.18.cloned.1.call-start = ((), (), s32[]{:S(2)}) async-start(), calls=%async_computation.13 | async-start | bytes 442368
  344.0 394.5 %all-reduce.3.cloned.1.call-start = ((), (), s32[]{:S(2)}) async-start(), calls=%async_computation.14 | async-start | bytes 3833856 | tf_op jit(solution)/shard_map/psum | solution.py:252
  345.7 249.8 %copy-start.17 = (f32[96,2304]{1,0:T(8,128)S(1)}, f32[96,2304]{1,0:T(8,128)}, u32[]{:S(2)}) copy-start(f32[96,2304]{1,0:T(8,128)} %param.32) | copy-start | bytes 2654212
  644.8 34.3 %copy-start.35 = (f32[12,96]{1,0:T(8,128)S(1)}, f32[12,96]{1,0:T(8,128)}, u32[]{:S(2)}) copy-start(f32[12,96]{1,0:T(8,128)} %param.36) | copy-start | bytes 13828
  (34 other events, 160.3 us)
Sparse Core Ops, SparseCore 0:
  10.2 29.1 all-gather.5
  41.6 68.3 all-gather.7
  112.2 53.3 all-gather.9
  254.1 37.3 reduce-scatter.9
  314.7 78.3 reduce-scatter.15
  395.3 97.8 reduce-scatter.13
  495.5 97.8 reduce-scatter.11
  595.6 39.8 all-gather.11
  638.4 29.5 reduce-scatter.17
  672.8 65.6 all-reduce.2
